TPU v7x, 32 devices: a whole 2x2x4 slice. The times are simulated.
32 devices in a mesh: grp: 2 (over y), row: 4 (over z), col: 4 (over x, core).
Axes of the slice: x: 2, y: 2, z: 4, core: 2. Of those that a mesh axis runs over, the one named last changes fastest.
Arguments:
- pair: bfloat16 [512, 256, 128], P(('grp', 'row'), 'col'), parts along dimension 0, may hold values from -6 to 6
- cotangent: bfloat16 [512, 256, 128], P(('grp', 'row'), 'col'), parts along dimension 0, may hold values from -6 to 6
- tile_mask: int32 [4, 2], P('grp'), parts along dimension 0, may hold values 0 or 1
- chain_ids: int32 [512], P('grp'), parts along dimension 0, may hold values from 0 to 4, never falling along the last dimension, each value on 1 to 128 neighbouring positions
- gain_in: float32 [2, 128], replicated, may hold values from 0.1 to 1.9
- weight_in: bfloat16 [2, 128, 512], replicated, may hold values from -0.5 to 0.5
- weight_gate: bfloat16 [2, 128, 128], replicated, may hold values from -0.5 to 0.5
- gain_out: float32 [2, 128], replicated, may hold values from 0.1 to 1.9
- weight_out: bfloat16 [2, 128, 128], replicated, may hold values from -0.5 to 0.5
Outputs:
- grad_pair: bfloat16 [512, 256, 128], P(('grp', 'row'), 'col'), parts along dimension 0
- grad_weight_in: float32 [4, 128, 512], P('grp'), parts along dimension 0
- grad_weight_gate: float32 [4, 128, 128], P('grp'), parts along dimension 0
- grad_weight_out: float32 [4, 128, 128], P('grp'), parts along dimension 0
- grad_gain_in: float32 [4, 128], P('grp'), parts along dimension 0
- grad_gain_out: float32 [4, 128], P('grp'), parts along dimension 0
There are 2 independent parts, one for each index of `grp`. A program takes and returns all parts, laid end to end along the dimension named above; an argument that names none is the same for every part. Nothing has to cross between parts.
Inputs may be any that keep to these rules, and one draw needn't show every extreme that they name: `chain_ids`: chain ids never fall along the tokens.
All inputs are finite; a program needn't handle non-finite values.
Results may differ from a plain program's by a relative error of at most 0.023.
Values may be sent and summed in bfloat16 or wider, within the bound.
A program may use at most 192 MiB of HBM per device.

v0:
```python
import functools

import jax
import jax.numpy as jnp
from jax import lax
from jax.experimental import pallas as pl
from jax.experimental.pallas import tpu as pltpu
from jax.sharding import PartitionSpec as P

eps = 1e-05
axes = ("row", "col")


def contract(a, b, dim_a, dim_b):
    return lax.dot_general(a, b, (((dim_a,), (dim_b,)), ((), ())), preferred_element_type=jnp.float32)


def layer_normalize(values):
    average = jnp.mean(values, axis=0, keepdims=True)
    centred = values - average
    inv_std = lax.rsqrt(jnp.mean(centred * centred, axis=0, keepdims=True) + eps)
    return (centred * inv_std, inv_std)


def norm_backward_step(grad_hat, normed, inv_std):
    inner = jnp.mean(grad_hat * normed, axis=0, keepdims=True)
    return inv_std * (grad_hat - jnp.mean(grad_hat, axis=0, keepdims=True) - normed * inner)


def front(cells, pair_mask, gain, weight_proj, weight_gating):
    zhat, inv_std = layer_normalize(cells)
    znorm = (zhat * gain[:, None]).astype(jnp.bfloat16)
    projected = contract(weight_proj, znorm, 0, 0)
    width = weight_proj.shape[1] // 4
    left_lin = projected[:width]
    left_gate = jax.nn.sigmoid(projected[width : 2 * width])
    right_lin = projected[2 * width : 3 * width]
    right_gate = jax.nn.sigmoid(projected[3 * width :])
    left = (pair_mask * left_gate * left_lin).astype(jnp.bfloat16)
    right = (right_gate * right_lin).astype(jnp.bfloat16)
    gating = jax.nn.sigmoid(contract(weight_gating, znorm, 0, 0))
    return (zhat, inv_std, znorm, left_lin, left_gate, right_lin, right_gate, left, right, gating)


def back_half(cells, tri, gating, gain, weight_final):
    xhat, inv_std = layer_normalize(tri)
    xnorm = (xhat * gain[:, None]).astype(jnp.bfloat16)
    update = contract(weight_final, xnorm, 0, 0)
    result = (cells + gating * update).astype(jnp.bfloat16)
    return (xhat, inv_std, xnorm, update, result)


def post_grad(incoming, gating, backs, gain, weight_final):
    xhat, inv_std, xnorm, update = backs[:4]
    grad_update = (incoming * gating).astype(jnp.bfloat16)
    grad_gating = (incoming * update * gating * (1.0 - gating)).astype(jnp.bfloat16)
    grad_wout = contract(xnorm, grad_update, 1, 1)
    grad_xnorm = contract(weight_final, grad_update, 1, 0)
    grad_gout = jnp.sum(grad_xnorm * xhat, axis=1)
    grad_tri = norm_backward_step(grad_xnorm * gain[:, None], xhat, inv_std).astype(jnp.bfloat16)
    return (grad_tri, grad_gating, grad_wout, grad_gout)


def pre_grad(
    incoming, grad_left, grad_right, grad_gating, fronts, pair_mask, gain, weight_proj, weight_gating
):
    zhat, inv_std, znorm, left_lin, left_gate, right_lin, right_gate = fronts[:7]
    masked = grad_left * pair_mask
    grad_proj = jnp.concatenate(
        [
            masked * left_gate,
            masked * left_lin * left_gate * (1.0 - left_gate),
            grad_right * right_gate,
            grad_right * right_lin * right_gate * (1.0 - right_gate),
        ],
        axis=0,
    ).astype(jnp.bfloat16)
    grad_win = contract(znorm, grad_proj, 1, 1)
    grad_wgate = contract(znorm, grad_gating, 1, 1)
    grad_znorm = contract(weight_proj, grad_proj, 1, 0)
    grad_znorm = grad_znorm + contract(weight_gating, grad_gating, 1, 0)
    grad_gin = jnp.sum(grad_znorm * zhat, axis=1)
    grad_input = incoming + norm_backward_step(grad_znorm * gain[:, None], zhat, inv_std)
    return (grad_input, grad_win, grad_wgate, grad_gin)


lanes = 128
half = lanes // 2


def swap_halves(even, odd):
    low = lax.broadcasted_iota(jnp.int32, even.shape, 1) < half
    return (
        jnp.where(low, even, pltpu.roll(odd, half, 1)),
        jnp.where(low, pltpu.roll(even, half, 1), odd),
    )


def unpack(x_ref, rows_ref):
    chunks = x_ref.shape[2] // lanes

    def step(p, _):
        for m in range(chunks):
            rows_ref[p, m * 16 : (m + 1) * 16, :] = x_ref[
                p, :, m * lanes : (m + 1) * lanes
            ].astype(jnp.float32)
        return 0

    lax.fori_loop(0, x_ref.shape[0], step, 0)


def pack(rows_ref, o_ref):
    chunks = o_ref.shape[2] // lanes

    def step(p, _):
        for m in range(chunks):
            o_ref[p, :, m * lanes : (m + 1) * lanes] = rows_ref[
                p, m * 16 : (m + 1) * 16, :
            ].astype(jnp.bfloat16)
        return 0

    lax.fori_loop(0, o_ref.shape[0], step, 0)


def row_sets(rows_ref, first, split):
    pairs = rows_ref.shape[1] // 16
    if split:
        return [pl.ds(first, pairs, stride=16), pl.ds(first + 8, pairs, stride=16)]
    return [pl.ds(first, pairs, stride=16)]


def gather_matrix(rows_ref, first, split, whole_ref, sides):
    grid_rows, grid_cols = sides
    for r in range(grid_rows):
        for c in range(grid_cols // 2):
            p = r * grid_cols + 2 * c
            sets = row_sets(rows_ref, first, split)
            a = jnp.concatenate([rows_ref[p, s, :] for s in sets], axis=0)
            b = jnp.concatenate([rows_ref[p + 1, s, :] for s in sets], axis=0)
            even, odd = swap_halves(a, b)
            rows = even.shape[0]
            whole_ref[c, pl.ds(2 * rows * r, rows, stride=2), :] = even
            whole_ref[c, pl.ds(2 * rows * r + 1, rows, stride=2), :] = odd
    return jnp.concatenate(
        [whole_ref[c].astype(jnp.bfloat16) for c in range(grid_cols // 2)], axis=1
    )


def scatter_matrix(values, whole_ref, rows_ref, first, split, sides):
    grid_rows, grid_cols = sides
    rows = values.shape[0] // grid_rows // 2
    for c in range(grid_cols // 2):
        whole_ref[c] = values[:, c * lanes : (c + 1) * lanes]
    for r in range(grid_rows):
        for c in range(grid_cols // 2):
            p = r * grid_cols + 2 * c
            even = whole_ref[c, pl.ds(2 * rows * r, rows, stride=2), :]
            odd = whole_ref[c, pl.ds(2 * rows * r + 1, rows, stride=2), :]
            blocks = swap_halves(even, odd)
            sets = row_sets(rows_ref, first, split)
            size = rows // len(sets)
            for n in range(2):
                for k, s in enumerate(sets):
                    rows_ref[p + n, s, :] = blocks[n][k * size : (k + 1) * size]


def forward_kernel(dims, sides, x_ref, o_ref, left_ref, right_ref, rows_in, rows_out, whole, whole2):
    unpack(x_ref, rows_in)

    def step(h, _):
        left = gather_matrix(rows_in, h, False, whole.at[0], sides)
        right = gather_matrix(rows_in, h + 8, False, whole.at[1], sides)
        left_ref[h] = left
        right_ref[h] = right
        scatter_matrix(contract(left, right, *dims), whole2.at[0], rows_out, h, True, sides)
        return 0

    lax.fori_loop(0, left_ref.shape[0], step, 0)
    pack(rows_out, o_ref)


def backward_kernel(
    outgoing, sides, x_ref, left_ref, right_ref, o_ref, rows_in, rows_out, whole, whole2
):
    unpack(x_ref, rows_in)

    def step(h, _):
        grad = gather_matrix(rows_in, h, True, whole.at[0], sides)
        left, right = left_ref[h], right_ref[h]
        if outgoing:
            grad_left, grad_right = contract(grad, right, 1, 0), contract(grad, left, 0, 0)
        else:
            grad_left, grad_right = contract(right, grad, 1, 1), contract(left, grad, 1, 0)
        scatter_matrix(grad_left, whole2.at[0], rows_out, h, False, sides)
        scatter_matrix(grad_right, whole2.at[1], rows_out, h + 8, False, sides)
        return 0

    lax.fori_loop(0, left_ref.shape[0], step, 0)
    pack(rows_out, o_ref)


def triangle_call(body, operands, out_shapes, peers, tokens, big_in, cells):
    wide, narrow = (peers, cells // lanes * 16, lanes), (peers, cells // lanes * 8, lanes)
    vmem = pl.BlockSpec(memory_space=pltpu.VMEM)
    square = pltpu.VMEM((2, tokens // lanes, tokens, lanes), jnp.float32)
    return pl.pallas_call(
        body,
        out_shape=out_shapes,
        in_specs=[vmem] * len(operands),
        out_specs=[vmem] * len(out_shapes),
        scratch_shapes=[
            pltpu.VMEM(wide if big_in else narrow, jnp.float32),
            pltpu.VMEM(narrow if big_in else wide, jnp.float32),
            square,
            square,
        ],
        compiler_params=pltpu.CompilerParams(vmem_limit_bytes=40 << 20),
    )(*operands)


def exchange_kernel(shared, *refs):
    count = len(shared)
    sources, targets = refs[:count], refs[count : 2 * count]
    send_sem, recv_sem, own_sem = refs[2 * count :]
    row, col, cols = lax.axis_index("row"), lax.axis_index("col"), lax.axis_size("col")
    peers = targets[0].shape[0]
    me = row * cols + col

    def device(d):
        q = lax.rem(me + d, peers)
        return q, {"row": q // cols, "col": lax.rem(q, cols)}

    barrier = pltpu.get_barrier_semaphore()
    for d in range(1, peers):
        pl.semaphore_signal(
            barrier, inc=1, device_id=device(d)[1], device_id_type=pl.DeviceIdType.MESH
        )
    pl.semaphore_wait(barrier, peers - 1)
    copies = []
    for n in range(count):
        for d in range(1, peers):
            q, target = device(d)
            copies.append(
                pltpu.make_async_remote_copy(
                    src_ref=sources[n] if shared[n] else sources[n].at[q],
                    dst_ref=targets[n].at[me],
                    send_sem=send_sem.at[n, d],
                    recv_sem=recv_sem.at[n, d],
                    device_id=target,
                    device_id_type=pl.DeviceIdType.MESH,
                )
            )
            copies[-1].start()
        copies.append(
            pltpu.make_async_copy(
                sources[n] if shared[n] else sources[n].at[me], targets[n].at[me], own_sem.at[n]
            )
        )
        copies[-1].start()
    for copy in copies:
        copy.wait()


def exchange_call(number, peers, operands, shared):
    count = len(operands)
    anywhere = pl.BlockSpec(memory_space=pl.ANY)
    outs = [
        jax.ShapeDtypeStruct((peers,) + x.shape[0 if one else 1 :], x.dtype)
        for x, one in zip(operands, shared)
    ]
    return pl.pallas_call(
        functools.partial(exchange_kernel, shared),
        out_shape=outs,
        in_specs=[anywhere] * count,
        out_specs=[anywhere] * count,
        scratch_shapes=[
            pltpu.SemaphoreType.DMA((count, peers)),
            pltpu.SemaphoreType.DMA((count, peers)),
            pltpu.SemaphoreType.DMA((count,)),
        ],
        compiler_params=pltpu.CompilerParams(collective_id=number, has_side_effects=True),
    )(*operands)


def local_mask(tile_mask, chain_ids, row_start, col_start, rows_dev, cols_dev):
    tile_count = tile_mask.shape[0]
    tile_size = chain_ids.shape[0] // tile_count
    row_ids = row_start + jnp.arange(rows_dev, dtype=jnp.int32)
    col_ids = col_start + jnp.arange(cols_dev, dtype=jnp.int32)
    tile_index = jnp.arange(tile_count, dtype=jnp.int32)
    row_hot = (row_ids[:, None] // tile_size == tile_index[None, :]).astype(jnp.float32)
    col_hot = (col_ids[:, None] // tile_size == tile_index[None, :]).astype(jnp.float32)
    tile_vals = jnp.dot(jnp.dot(row_hot, tile_mask.astype(jnp.float32)), col_hot.T)
    row_chain = lax.dynamic_slice_in_dim(chain_ids, row_start, rows_dev)
    col_chain = lax.dynamic_slice_in_dim(chain_ids, col_start, cols_dev)
    same_chain = (row_chain[:, None] == col_chain[None, :]).astype(jnp.float32)
    return jnp.maximum(tile_vals, same_chain).reshape(1, -1)


def per_device(
    pair, cotangent, tile_mask, chain_ids, gain_in, weight_in, weight_gate, gain_out, weight_out
):
    rows_dev, cols_dev, channels = pair.shape
    hidden = weight_out.shape[1]
    grid_rows, grid_cols = lax.axis_size("row"), lax.axis_size("col")
    peers = grid_rows * grid_cols
    share = hidden // peers
    tokens = rows_dev * grid_rows
    cells_dev = rows_dev * cols_dev

    def triangle(spec, a, b):
        return jnp.einsum(spec, a, b, preferred_element_type=jnp.float32)

    numbers = {}

    def exchange(*operands, shared=()):
        shared = shared or (False,) * len(operands)
        if kernels:
            key = (shared,) + tuple(x.shape for x in operands)
            number = numbers.setdefault(key, len(numbers))
            return exchange_call(number, peers, operands, shared)
        return [
            lax.all_to_all(jnp.broadcast_to(x, (peers,) + x.shape) if one else x, axes, 0, 0)
            for x, one in zip(operands, shared)
        ]

    kernels = share == 8 and cols_dev == half and rows_dev == half and grid_cols % 2 == 0
    sides = (grid_rows, grid_cols)
    whole_grid = (share, tokens, tokens)

    def spread(*arrays):
        sent = [a.reshape(peers, share, cells_dev) for a in arrays]
        if len(arrays) == 2 or not kernels:
            return jnp.concatenate(sent, axis=1)
        halves = sent[0].reshape(peers, share, 2, -1).transpose(0, 2, 1, 3)
        return halves.reshape(peers, 2 * share, -1)

    def collect(got, count):
        got = got.astype(jnp.float32)
        if count == 1 and kernels:
            got = got.reshape(peers, 2, share, -1).transpose(0, 2, 1, 3)
            return [got.reshape(hidden, cells_dev)]
        got = got.reshape(peers, count, share, cells_dev)
        return [got[:, n].reshape(hidden, cells_dev) for n in range(count)]

    def assemble(got, count):
        got = got.reshape(grid_rows, grid_cols, count * share, rows_dev, cols_dev)
        whole = got.transpose(2, 0, 3, 1, 4).reshape(count * share, tokens, tokens)
        return [whole[n * share : (n + 1) * share] for n in range(count)]

    def divide(*arrays):
        stacked = jnp.concatenate([a.astype(jnp.bfloat16) for a in arrays], axis=0)
        split = stacked.reshape(-1, grid_rows, rows_dev, grid_cols, cols_dev)
        return split.transpose(1, 3, 0, 2, 4).reshape(peers, -1, cells_dev)

    def shapes(*dims):
        return [jax.ShapeDtypeStruct(d, jnp.bfloat16) for d in dims]

    def forward_triangle(left, right, outgoing):
        (got,) = exchange(spread(left, right))
        if kernels:
            dims = (1, 1) if outgoing else (0, 0)
            blocks, left_all, right_all = triangle_call(
                functools.partial(forward_kernel, dims, sides),
                [got],
                shapes((peers, 16, cells_dev // 2), whole_grid, whole_grid),
                peers,
                tokens,
                True,
                cells_dev,
            )
        else:
            left_all, right_all = assemble(got, 2)
            spec = "hik,hjk->hij" if outgoing else "hki,hkj->hij"
            blocks = divide(triangle(spec, left_all, right_all))
        (got,) = exchange(blocks)
        return collect(got, 1)[0], left_all, right_all

    def backward_triangle(grad, left_all, right_all, outgoing, extra=()):
        got, *parts = exchange(spread(grad), *extra)
        if kernels:
            (blocks,) = triangle_call(
                functools.partial(backward_kernel, outgoing, sides),
                [got, left_all, right_all],
                shapes((peers, 16, cells_dev)),
                peers,
                tokens,
                False,
                cells_dev,
            )
        else:
            (whole,) = assemble(got, 1)
            if outgoing:
                grads = ("hij,hjk->hik", whole, right_all), ("hij,hik->hjk", whole, left_all)
            else:
                grads = ("hkj,hij->hki", right_all, whole), ("hki,hij->hkj", left_all, whole)
            blocks = divide(*[triangle(*g) for g in grads])
        sums = [add_parts(p) for p in parts]
        got, *totals = exchange(blocks, *sums, shared=(False,) + (True,) * len(sums))
        return collect(got, 2) + [t.reshape(-1, hidden) for t in totals]

    factor = 1.0 / tokens

    def stack_parts(weights, gains):
        blocks = [w[:, n : n + hidden] for w in weights for n in range(0, w.shape[1], hidden)]
        rows = jnp.concatenate(blocks + [g[None] for g in gains], axis=0) * factor
        rows = jnp.pad(rows, ((0, -rows.shape[0] % (16 * peers)), (0, 0)))
        return rows.astype(jnp.bfloat16).reshape(peers, -1, hidden)

    def add_parts(parts):
        return jnp.sum(parts.astype(jnp.float32), axis=0).astype(jnp.bfloat16)

    row_start = lax.axis_index("row") * rows_dev
    col_start = lax.axis_index("col") * cols_dev
    pair_mask = local_mask(tile_mask, chain_ids, row_start, col_start, rows_dev, cols_dev)
    cells_one = pair.reshape(-1, channels).T.astype(jnp.float32)
    front_one = front(cells_one, pair_mask, gain_in[0], weight_in[0], weight_gate[0])
    tri_one, left_one, right_one = forward_triangle(front_one[7], front_one[8], True)
    back_one = back_half(cells_one, tri_one, front_one[9], gain_out[0], weight_out[0])
    cells_two = back_one[4].astype(jnp.float32)
    front_two = front(cells_two, pair_mask, gain_in[1], weight_in[1], weight_gate[1])
    tri_two, left_two, right_two = forward_triangle(front_two[7], front_two[8], False)
    back_two = back_half(cells_two, tri_two, front_two[9], gain_out[1], weight_out[1])
    cot_two = cotangent.reshape(-1, channels).T.astype(jnp.float32)
    post_two = post_grad(cot_two, front_two[9], back_two, gain_out[1], weight_out[1])
    dleft_two, dright_two = backward_triangle(post_two[0], left_two, right_two, False)
    pre_two = pre_grad(
        cot_two,
        dleft_two,
        dright_two,
        post_two[1],
        front_two,
        pair_mask,
        gain_in[1],
        weight_in[1],
        weight_gate[1],
    )
    cot_one = pre_two[0].astype(jnp.bfloat16).astype(jnp.float32)
    post_one = post_grad(cot_one, front_one[9], back_one, gain_out[0], weight_out[0])
    early = stack_parts(
        (pre_two[1], pre_two[2], post_two[2], post_one[2]), (pre_two[3], post_two[3], post_one[3])
    )
    dleft_one, dright_one, early = backward_triangle(
        post_one[0], left_one, right_one, True, (early,)
    )
    pre_one = pre_grad(
        cot_one,
        dleft_one,
        dright_one,
        post_one[1],
        front_one,
        pair_mask,
        gain_in[0],
        weight_in[0],
        weight_gate[0],
    )
    grad_pair = pre_one[0].astype(jnp.bfloat16).T.reshape(rows_dev, cols_dev, channels)

    (parts,) = exchange(stack_parts((pre_one[1], pre_one[2]), (pre_one[3],)))
    (late,) = exchange(add_parts(parts), shared=(True,))
    early = early.astype(jnp.float32)
    late = late.reshape(-1, hidden).astype(jnp.float32)

    def block(rows, n, count=1):
        blocks = rows[n * channels : (n + count) * channels].reshape(count, channels, hidden)
        return jnp.concatenate([blocks[k] for k in range(count)], axis=1)

    return (
        grad_pair,
        jnp.stack([block(late, 0, 4), block(early, 0, 4)]),
        jnp.stack([block(late, 4), block(early, 4)]),
        jnp.stack([block(early, 6), block(early, 5)]),
        jnp.stack([late[5 * channels], early[7 * channels]]),
        jnp.stack([early[7 * channels + 2], early[7 * channels + 1]]),
    )


def solution(mesh):
    in_specs = (
        P(("grp", "row"), "col", None),
        P(("grp", "row"), "col", None),
        P("grp", None),
        P("grp"),
        P(),
        P(),
        P(),
        P(),
        P(),
    )
    out_specs = (
        P(("grp", "row"), "col", None),
        P("grp", None, None),
        P("grp", None, None),
        P("grp", None, None),
        P("grp", None),
        P("grp", None),
    )
    return jax.shard_map(
        per_device, mesh=mesh, in_specs=in_specs, out_specs=out_specs, check_vma=False
    )
```

profile of v0, /device:TPU:0, one launch (start us, length us, event | category | flops | bytes accessed | tf_op | source)
XLA Modules:
  0.0 519.0 jit_solution(14316436836184920254)
XLA Ops:
  20.2 2.8 pad_maximum_fusion.2.refs_0_
  23.0 40.9 %shard_map.136.x_ref = bf16[16,16,4096]{2,1,0:T(8,128)(2,1)} custom-call(bf16[16,16,4096]{2,1,0:T(8,128)(2,1)} %pad_maximum_fusion.2.refs_0_), custom_call_target="tpu_custom_call" | custom-call | tf_op jit(solution)/shard_map/pallas_call | solution.py:271
  65.5 5.6 %shard_map.137 = (bf16[16,16,2048]{2,1,0:T(8,128)(2,1)S(1)}, bf16[8,256,256]{2,1,0:T(8,128)(2,1)S(1)}, bf16[8,256,256]{2,1,0:T(8,128)(2,1)S(1)}) custom-call(bf16[16,16,4096]{2,1,0:T(8,128)(2,1)S(1)} %copy-done.1), custom_call_target="tpu_custom_call" | custom-call | tf_op jit(solution)/shard_map/pallas_call | solution.py:206
  72.1 33.0 %shard_map.138 = bf16[16,16,2048]{2,1,0:T(8,128)(2,1)} custom-call(bf16[16,16,2048]{2,1,0:T(8,128)(2,1)} %copy-done.8), custom_call_target="tpu_custom_call" | custom-call | tf_op jit(solution)/shard_map/pallas_call | solution.py:271
  115.5 3.8 fusion.29
  120.6 2.5 multiply_convert_fusion.14
  127.8 3.2 pad_maximum_fusion.3.refs_0_
  131.0 44.2 %shard_map.139.x_ref = bf16[16,16,4096]{2,1,0:T(8,128)(2,1)} custom-call(bf16[16,16,4096]{2,1,0:T(8,128)(2,1)} %pad_maximum_fusion.3.refs_0_), custom_call_target="tpu_custom_call" | custom-call | tf_op jit(solution)/shard_map/pallas_call | solution.py:271
  176.8 5.9 %shard_map.140 = (bf16[16,16,2048]{2,1,0:T(8,128)(2,1)S(1)}, bf16[8,256,256]{2,1,0:T(8,128)(2,1)S(1)}, bf16[8,256,256]{2,1,0:T(8,128)(2,1)S(1)}) custom-call(bf16[16,16,4096]{2,1,0:T(8,128)(2,1)S(1)} %copy-done.2), custom_call_target="tpu_custom_call" | custom-call | tf_op jit(solution)/shard_map/pallas_call | solution.py:206
  184.7 33.0 %shard_map.141 = bf16[16,16,2048]{2,1,0:T(8,128)(2,1)} custom-call(bf16[16,16,2048]{2,1,0:T(8,128)(2,1)} %copy-done.9), custom_call_target="tpu_custom_call" | custom-call | tf_op jit(solution)/shard_map/pallas_call | solution.py:271
  230.9 27.3 %shard_map.142.x_ref = bf16[16,16,2048]{2,1,0:T(8,128)(2,1)} custom-call(bf16[16,16,2048]{2,1,0:T(8,128)(2,1)} %bitcast.300), custom_call_target="tpu_custom_call" | custom-call | tf_op jit(solution)/shard_map/pallas_call | solution.py:271
  260.7 5.6 %shard_map.143.refs_0_ = bf16[16,16,4096]{2,1,0:T(8,128)(2,1)S(1)} custom-call(bf16[16,16,2048]{2,1,0:T(8,128)(2,1)S(1)} %copy-done.4, bf16[8,256,256]{2,1,0:T(8,128)(2,1)S(1)} %get-tuple-element.18.left_ref, bf16[8,256,256]{2,1,0:T(8,128)(2,1)S(1)} %copy-done.6), custom_call_target="tpu_custom_call" | custom-call | tf_op jit(solution)/shard_map/pallas_call | solution.py:206
  267.6 44.2 %shard_map.144 = bf16[16,16,4096]{2,1,0:T(8,128)(2,1)} custom-call(bf16[16,16,4096]{2,1,0:T(8,128)(2,1)} %copy-done.3), custom_call_target="tpu_custom_call" | custom-call | tf_op jit(solution)/shard_map/pallas_call | solution.py:271
  313.9 2.3 slice_bitcast_fusion.3
  316.3 3.0 copy.32
  319.2 2.9 copy.34
  322.1 5.9 %multiply_convert_fusion.11 = (bf16[128,4096]{0,1:T(8,128)(2,1)S(1)}, bf16[128,4096]{0,1:T(8,128)(2,1)S(1)}, bf16[128,4096]{0,1:T(8,128)(2,1)S(1)}, bf16[128,4096]{0,1:T(8,128)(2,1)S(1)}) fusion(f32[128,4096]{0,1:T(8,128)} %copy.32, f32[4096]{0:T(1024)S(1)} %mul.388, f32[512,4096]{0,1:T(8,128)} %copy-done.10, f32[128,4096]{0,1:T(8,128)} %copy.34), kind=kLoop, calls=%fused_computation.118 | loop fusion | flops 11010048 | bytes 16793600 | tf_op jit(solution)/shard_map/convert.21
  331.2 2.4 fusion.23
  334.4 4.3 fusion.28
  339.3 2.6 multiply_reduce_fusion
  341.9 9.0 %concatenate.29 = f32[899,128]{1,0:T(8,128)} concatenate(f32[128,128]{1,0:T(8,128)} %get-tuple-element.82, f32[128,128]{1,0:T(8,128)} %get-tuple-element.81, f32[128,128]{1,0:T(8,128)} %get-tuple-element.80, f32[128,128]{1,0:T(8,128)S(1)} %get-tuple-element.79, f32[128,128]{1,0:T(8,128)} %fusion.119, f32[128,128]{1,0:T(8,128)S(1)} %copy-done.45, f32[128,128]{1,0:T(8,128)S(1)} %fusion.70, ...), dimensions={0} | concatenate | bytes 920576 | tf_op jit(solution)/shard_map/concatenate | solution.py:406
  352.0 3.8 multiply_convert_fusion.6
  356.5 43.3 %shard_map.145 = (bf16[16,16,2048]{2,1,0:T(8,128)(2,1)}, bf16[16,64,128]{2,1,0:T(8,128)(2,1)}) custom-call(bf16[16,16,2048]{2,1,0:T(8,128)(2,1)} %bitcast.299, bf16[16,64,128]{2,1,0:T(8,128)(2,1)} %bitcast.306), custom_call_target="tpu_custom_call" | custom-call | tf_op jit(solution)/shard_map/pallas_call | solution.py:271
  401.1 5.7 %shard_map.146.refs_0_ = bf16[16,16,4096]{2,1,0:T(8,128)(2,1)S(1)} custom-call(bf16[16,16,2048]{2,1,0:T(8,128)(2,1)S(1)} %copy-done.7, bf16[8,256,256]{2,1,0:T(8,128)(2,1)S(1)} %get-tuple-element.21.left_ref, bf16[8,256,256]{2,1,0:T(8,128)(2,1)S(1)} %get-tuple-element.22.right_ref), custom_call_target="tpu_custom_call" | custom-call | tf_op jit(solution)/shard_map/pallas_call | solution.py:206
  408.7 56.1 %shard_map.147 = (bf16[16,16,4096]{2,1,0:T(8,128)(2,1)}, bf16[16,64,128]{2,1,0:T(8,128)(2,1)}) custom-call(bf16[16,16,4096]{2,1,0:T(8,128)(2,1)} %copy-done, bf16[64,128]{1,0:T(8,128)(2,1)} %reduce_sum.221.refs_1_), custom_call_target="tpu_custom_call" | custom-call | tf_op jit(solution)/shard_map/pallas_call | solution.py:271
  469.2 2.3 slice_bitcast_fusion.1
  473.4 2.9 copy.39
  476.3 5.4 %multiply_convert_fusion.3 = (bf16[128,4096]{0,1:T(8,128)(2,1)S(1)}, bf16[128,4096]{0,1:T(8,128)(2,1)S(1)}, bf16[128,4096]{0,1:T(8,128)(2,1)S(1)}, bf16[128,4096]{0,1:T(8,128)(2,1)S(1)}) fusion(f32[128,4096]{0,1:T(8,128)S(1)} %copy.37, f32[4096]{0:T(1024)S(1)} %mul.388, f32[512,4096]{0,1:T(8,128)} %copy-done.11, f32[128,4096]{0,1:T(8,128)} %copy.39), kind=kLoop, calls=%fused_computation.106 | loop fusion | flops 11010048 | bytes 16793600 | tf_op jit(solution)/shard_map/convert.15
  484.3 2.3 fusion.44
  487.1 6.1 %fusion.59 = bf16[4096,128]{1,0:T(8,128)(2,1)} fusion(bf16[64,64,128]{2,1,0:T(8,128)(2,1)S(1)} %copy-done.13, f32[4096,128]{1,0:T(8,128)S(1)} %get-tuple-element.103, f32[4096,128]{1,0:T(8,128)S(1)} %copy-done.22, f32[4096,128]{1,0:T(8,128)S(1)} %copy-done.24, f32[4096,128]{1,0:T(8,128)S(1)} %copy-done.26, f32[4096]{0:T(1024)S(1)} %broadcast_multiply_fusion.3, ...), kind=kLoop, calls=%fused_computation.101 | loop fusion | flops 13107200 | bytes 11666432 | tf_op jit(solution)/shard_map/convert_element_type | solution.py:457
  494.5 9.9 %shard_map.148 = bf16[16,48,128]{2,1,0:T(8,128)(2,1)} custom-call(bf16[16,48,128]{2,1,0:T(8,128)(2,1)} %bitcast.307), custom_call_target="tpu_custom_call" | custom-call | tf_op jit(solution)/shard_map/pallas_call | solution.py:271
  505.9 9.5 %shard_map.149 = bf16[16,48,128]{2,1,0:T(8,128)(2,1)} custom-call(bf16[48,128]{1,0:T(8,128)(2,1)} %reduce_sum.225.refs_0_), custom_call_target="tpu_custom_call" | custom-call | tf_op jit(solution)/shard_map/pallas_call | solution.py:271
  (217 shorter events, 85.4 us)
Async XLA Ops:
  0.6 7.8 %copy-start.12 = (bf16[64,64,128]{2,1,0:T(8,128)(2,1)S(1)}, bf16[64,64,128]{2,1,0:T(8,128)(2,1)}, u32[]{:S(2)}) copy-start(bf16[64,64,128]{2,1,0:T(8,128)(2,1)} %param.9) | copy-start | bytes 3145732
  2.8 7.0 %copy-start.61 = (f32[128]{0:T(128)}, f32[128]{0:T(128)S(1)}, u32[]{:S(2)}) copy-start(f32[128]{0:T(128)S(1)} %get-tuple-element.94) | copy-start | bytes 1540
  6.5 4.5 copy-start.50
  14.3 3.2 copy-start.11
  72.1 37.3 %copy-start.54 = (f32[16,8]{1,0:T(8,128)S(1)}, f32[16,8]{1,0:T(8,128)}, u32[]{:S(2)}) copy-start(f32[16,8]{1,0:T(8,128)} %mul.396) | copy-start | bytes 1540
  105.1 4.3 copy-start.19
  112.1 3.3 copy-start.29
  112.1 3.4 copy-start.51
  112.1 3.4 copy-start.55
  114.2 5.2 copy-start.15
  120.6 3.5 copy-start.10
  217.7 3.2 copy-start.18
  217.7 4.2 copy-start.30
  217.7 4.2 copy-start.38
  322.1 5.9 %copy-start.17 = (bf16[128,4096]{0,1:T(8,128)(2,1)S(1)}, bf16[128,4096]{0,1:T(8,128)(2,1)}, u32[]{:S(2)}) copy-start(bf16[128,4096]{0,1:T(8,128)(2,1)} %copy-done.15) | copy-start | bytes 3145732
  322.1 5.9 %copy-start.57 = (f32[128]{0:T(128)S(1)}, f32[128]{0:T(128)}, u32[]{:S(2)}) copy-start(f32[128]{0:T(128)} %get-tuple-element.93) | copy-start | bytes 1540
  331.2 3.2 copy-start.21
  331.2 3.2 copy-start.23
  331.2 3.2 copy-start.31
  333.6 5.1 copy-start.25
  334.3 4.3 copy-start.46
  334.4 4.3 copy-start.48
  334.4 4.3 copy-start.14
  334.4 4.3 copy-start.42
  334.4 4.3 copy-start.43
  334.4 4.3 copy-start.59
  401.1 7.0 %copy-start.44 = (bf16[16,64,128]{2,1,0:T(8,128)(2,1)S(1)}, bf16[16,64,128]{2,1,0:T(8,128)(2,1)}, u32[]{:S(2)}) copy-start(bf16[16,64,128]{2,1,0:T(8,128)(2,1)} %get-tuple-element.23) | copy-start | bytes 786436
  464.9 3.9 copy-start.37
  476.3 5.4 %copy-start.28 = (bf16[128,4096]{0,1:T(8,128)(2,1)S(1)}, bf16[128,4096]{0,1:T(8,128)(2,1)}, u32[]{:S(2)}) copy-start(bf16[128,4096]{0,1:T(8,128)(2,1)} %copy-done.27) | copy-start | bytes 3145732
  484.2 2.9 copy-start.26
  484.2 2.8 copy-start.47
  493.7 23.4 %copy-start.63 = (f32[1,128]{1,0:T(1,128)S(1)}, f32[1,128]{1,0:T(1,128)}, u32[]{:S(2)}) copy-start(f32[1,128]{1,0:T(1,128)} %get-tuple-element.66) | copy-start | bytes 1540
  (32 other events, 52.6 us)
where the time goes:
time: 529 us; the launch traced here: 519 us
  Pallas kernels  364 us (69%)
  other arithmetic  62.8 us (12%)
  local copies, waits for them, and re-layouts  59.6 us (11%)
  matrix products  30.4 us (6%)
    pallas_call x10, Pallas kernels, exchange_call(): pl.pallas_call(functools.partial(exchange_kernel, shared), out_shape=outs...  341 us
    dot_general x18, matrix products, contract(): lax.dot_general(a, b, (((dim_a,), (dim_b,)), ((), ())), preferred_element...  29.4 us
    pallas_call x4, Pallas kernels, triangle_call(): pl.pallas_call(body, out_shape=out_shapes, in_specs=[vmem] * len(operands...  22.7 us
    unnamed x136, local copies, waits for them, and re-layouts  20.1 us
    another operation x6, local copies, waits for them, and re-layouts, collect(): return [got[:, n].reshape(hidden, cells_dev) for n in range(count)]  15.3 us
    another operation x4, other arithmetic  12.4 us

commit v1 on v0

--- a/solution.py
+++ b/solution.py
@@ -313,9 +313,9 @@
 
     numbers = {}
 
-    def exchange(*operands, shared=()):
+    def exchange(*operands, shared=(), direct=True):
         shared = shared or (False,) * len(operands)
-        if kernels:
+        if kernels and direct:
             key = (shared,) + tuple(x.shape for x in operands)
             number = numbers.setdefault(key, len(numbers))
             return exchange_call(number, peers, operands, shared)
@@ -336,12 +336,13 @@
         return halves.reshape(peers, 2 * share, -1)
 
     def collect(got, count):
-        got = got.astype(jnp.float32)
         if count == 1 and kernels:
             got = got.reshape(peers, 2, share, -1).transpose(0, 2, 1, 3)
-            return [got.reshape(hidden, cells_dev)]
+            return [got.reshape(hidden, cells_dev).astype(jnp.float32)]
         got = got.reshape(peers, count, share, cells_dev)
-        return [got[:, n].reshape(hidden, cells_dev) for n in range(count)]
+        return [
+            got[:, n].reshape(hidden, cells_dev).astype(jnp.float32) for n in range(count)
+        ]
 
     def assemble(got, count):
         got = got.reshape(grid_rows, grid_cols, count * share, rows_dev, cols_dev)
@@ -373,11 +374,11 @@
             left_all, right_all = assemble(got, 2)
             spec = "hik,hjk->hij" if outgoing else "hki,hkj->hij"
             blocks = divide(triangle(spec, left_all, right_all))
-        (got,) = exchange(blocks)
+        (got,) = exchange(blocks, direct=False)
         return collect(got, 1)[0], left_all, right_all
 
-    def backward_triangle(grad, left_all, right_all, outgoing, extra=()):
-        got, *parts = exchange(spread(grad), *extra)
+    def backward_triangle(grad, left_all, right_all, outgoing):
+        (got,) = exchange(spread(grad))
         if kernels:
             (blocks,) = triangle_call(
                 functools.partial(backward_kernel, outgoing, sides),
@@ -395,16 +396,15 @@
             else:
                 grads = ("hkj,hij->hki", right_all, whole), ("hki,hij->hkj", left_all, whole)
             blocks = divide(*[triangle(*g) for g in grads])
-        sums = [add_parts(p) for p in parts]
-        got, *totals = exchange(blocks, *sums, shared=(False,) + (True,) * len(sums))
-        return collect(got, 2) + [t.reshape(-1, hidden) for t in totals]
+        (got,) = exchange(blocks, direct=False)
+        return collect(got, 2)
 
     factor = 1.0 / tokens
 
     def stack_parts(weights, gains):
         blocks = [w[:, n : n + hidden] for w in weights for n in range(0, w.shape[1], hidden)]
         rows = jnp.concatenate(blocks + [g[None] for g in gains], axis=0) * factor
-        rows = jnp.pad(rows, ((0, -rows.shape[0] % (16 * peers)), (0, 0)))
+        rows = jnp.pad(rows, ((0, -rows.shape[0] % peers), (0, 0)))
         return rows.astype(jnp.bfloat16).reshape(peers, -1, hidden)
 
     def add_parts(parts):
@@ -437,12 +437,7 @@
     )
     cot_one = pre_two[0].astype(jnp.bfloat16).astype(jnp.float32)
     post_one = post_grad(cot_one, front_one[9], back_one, gain_out[0], weight_out[0])
-    early = stack_parts(
-        (pre_two[1], pre_two[2], post_two[2], post_one[2]), (pre_two[3], post_two[3], post_one[3])
-    )
-    dleft_one, dright_one, early = backward_triangle(
-        post_one[0], left_one, right_one, True, (early,)
-    )
+    dleft_one, dright_one = backward_triangle(post_one[0], left_one, right_one, True)
     pre_one = pre_grad(
         cot_one,
         dleft_one,
@@ -456,22 +451,22 @@
     )
     grad_pair = pre_one[0].astype(jnp.bfloat16).T.reshape(rows_dev, cols_dev, channels)
 
-    (parts,) = exchange(stack_parts((pre_one[1], pre_one[2]), (pre_one[3],)))
-    (late,) = exchange(add_parts(parts), shared=(True,))
-    early = early.astype(jnp.float32)
-    late = late.reshape(-1, hidden).astype(jnp.float32)
-
-    def block(rows, n, count=1):
-        blocks = rows[n * channels : (n + count) * channels].reshape(count, channels, hidden)
-        return jnp.concatenate([blocks[k] for k in range(count)], axis=1)
-
+    stacked = stack_parts(
+        (pre_one[1], pre_one[2], post_one[2], pre_two[1], pre_two[2], post_two[2]),
+        (pre_one[3], pre_two[3], post_one[3], post_two[3]),
+    )
+    (parts,) = exchange(stacked, direct=False)
+    (totals,) = exchange(add_parts(parts), shared=(True,), direct=False)
+    totals = totals.reshape(-1, hidden).astype(jnp.float32)
+    blocks = totals[: 12 * channels].reshape(2, 6, channels, hidden)
+    gains = totals[12 * channels :]
     return (
         grad_pair,
-        jnp.stack([block(late, 0, 4), block(early, 0, 4)]),
-        jnp.stack([block(late, 4), block(early, 4)]),
-        jnp.stack([block(early, 6), block(early, 5)]),
-        jnp.stack([late[5 * channels], early[7 * channels]]),
-        jnp.stack([early[7 * channels + 2], early[7 * channels + 1]]),
+        jnp.concatenate([blocks[:, n] for n in range(4)], axis=2),
+        blocks[:, 4],
+        blocks[:, 5],
+        gains[:2],
+        gains[2:4],
     )
 
 

time: 529 us -> 498 us (0.941)
  Pallas kernels: 364 us -> 159 us
  waiting for transfers between devices: 0 us -> 117 us
  starting transfers between devices: 0 us -> 69.9 us
  local copies, waits for them, and re-layouts: 59.6 us -> 41.6 us
    pallas_call x10 -> x4, Pallas kernels: 341 us -> 133 us  [exchange_call(): pl.pallas_call(functools.partial(exchange_kernel, shared), out_shape=outs...]
    all_to_all x0 -> x6, waiting for transfers between devices: none -> 117 us  [exchange(): lax.all_to_all(jnp.broadcast_to(x, (peers,) + x.shape) if one else x, axe...]
    all_to_all x0 -> x6, starting transfers between devices: none -> 69.9 us  [exchange(): lax.all_to_all(jnp.broadcast_to(x, (peers,) + x.shape) if one else x, axe...]
    another operation x7 -> x0, local copies, waits for them, and re-layouts: 15.4 us -> none  [the longest x6 15.3 us: collect(): return [got[:, n].reshape(hidden, cells_dev) for n in range(count)]]
    convert_element_type x0 -> x5, local copies, waits for them, and re-layouts: none -> 10.7 us  [the longest x4 10.6 us: collect(): got[:, n].reshape(hidden, cells_dev).astype(jnp.float32)]
    convert_element_type x2 -> x4, other arithmetic: 1.95 us -> 11.8 us  [the longest x2 7.33 us: collect(): got[:, n].reshape(hidden, cells_dev).astype(jnp.float32)]
    concatenate x2 -> x1, local copies, waits for them, and re-layouts: 9.06 us -> 0.08 us  [stack_parts(): rows = jnp.concatenate(blocks + [g[None] for g in gains], axis=0) * factor]
    another operation x11 -> x3, other arithmetic: 15.7 us -> 11.4 us
  transfers between devices with their start and end apart: 0 -> 6, of which waited for: 0 -> 6; matrix products, arithmetic and copies ran while one was open for 0% -> 7% of each run, Pallas kernels for 0% -> 0%
where the time goes in v1:
time: 498 us; the launch traced here: 492 us
  Pallas kernels  159 us (32%)
  waiting for transfers between devices  117 us (23%)
  starting transfers between devices  69.9 us (14%)
  other arithmetic  67.1 us (13%)
  local copies, waits for them, and re-layouts  41.6 us (8%)
  matrix products  35.5 us (7%)
    pallas_call x4, Pallas kernels, exchange_call(): pl.pallas_call(functools.partial(exchange_kernel, shared), out_shape=outs...  133 us
    all_to_all x6, waiting for transfers between devices, exchange(): lax.all_to_all(jnp.broadcast_to(x, (peers,) + x.shape) if one else x, axe...  117 us
    all_to_all x6, starting transfers between devices, exchange(): lax.all_to_all(jnp.broadcast_to(x, (peers,) + x.shape) if one else x, axe...  69.9 us
    dot_general x18, matrix products, contract(): lax.dot_general(a, b, (((dim_a,), (dim_b,)), ((), ())), preferred_element...  34.5 us
    pallas_call x4, Pallas kernels, triangle_call(): pl.pallas_call(body, out_shape=out_shapes, in_specs=[vmem] * len(operands...  26.4 us
    unnamed x172, local copies, waits for them, and re-layouts  18 us
    another operation x3, other arithmetic  11.4 us
    convert_element_type x4, local copies, waits for them, and re-layouts, collect(): got[:, n].reshape(hidden, cells_dev).astype(jnp.float32)  10.6 us
  transfers between devices with their start and end apart: 6, of which 6 were waited for; matrix products, arithmetic and copies ran while one was open for 7% of the time, Pallas kernels for 0%

profile of v1, /device:TPU:0, one launch (start us, length us, event | category | flops | bytes accessed | tf_op | source)
XLA Modules:
  0.0 492.4 jit_solution(8988397967094952776)
XLA Ops:
  18.5 40.9 %shard_map.136.x_ref = bf16[16,16,4096]{2,1,0:T(8,128)(2,1)} custom-call(bf16[16,16,4096]{2,1,0:T(8,128)(2,1)} %pad_maximum_fusion.2.refs_0_), custom_call_target="tpu_custom_call" | custom-call | tf_op jit(solution)/shard_map/pallas_call | solution.py:271
  61.0 6.6 %shard_map.137 = (bf16[16,16,2048]{2,1,0:T(8,128)(2,1)}, bf16[8,256,256]{2,1,0:T(8,128)(2,1)S(1)}, bf16[8,256,256]{2,1,0:T(8,128)(2,1)S(1)}) custom-call(bf16[16,16,4096]{2,1,0:T(8,128)(2,1)S(1)} %copy-done), custom_call_target="tpu_custom_call" | custom-call | tf_op jit(solution)/shard_map/pallas_call | solution.py:206
  67.6 16.5 %all-to-all-start = ((bf16[16,16,2048]{2,1,0:T(8,128)(2,1)}), bf16[16,16,2048]{2,1,0:T(8,128)(2,1)}, u32[]{:S(2)}, u32[]{:S(2)}) async-start(bf16[16,16,2048]{2,1,0:T(8,128)(2,1)} %get-tuple-element.12), calls=%async_computation | async-start | bytes 2097152 | tf_op jit(solution)/shard_map/all_to_all | solution.py:323
  86.0 3.3 fusion.9
  89.3 17.9 %all-to-all-done = bf16[16,16,2048]{2,1,0:T(8,128)(2,1)} async-done(((bf16[16,16,2048]{2,1,0:T(8,128)(2,1)}), bf16[16,16,2048]{2,1,0:T(8,128)(2,1)}, u32[]{:S(2)}, u32[]{:S(2)}) %all-to-all-start) | async-done | bytes 1048608 | tf_op jit(solution)/shard_map/all_to_all | solution.py:323
  125.1 3.1 pad_maximum_fusion.3.refs_0_
  128.2 40.4 %shard_map.138.x_ref = bf16[16,16,4096]{2,1,0:T(8,128)(2,1)} custom-call(bf16[16,16,4096]{2,1,0:T(8,128)(2,1)} %pad_maximum_fusion.3.refs_0_), custom_call_target="tpu_custom_call" | custom-call | tf_op jit(solution)/shard_map/pallas_call | solution.py:271
  170.2 5.9 %shard_map.139 = (bf16[16,16,2048]{2,1,0:T(8,128)(2,1)S(1)}, bf16[8,256,256]{2,1,0:T(8,128)(2,1)S(1)}, bf16[8,256,256]{2,1,0:T(8,128)(2,1)S(1)}) custom-call(bf16[16,16,4096]{2,1,0:T(8,128)(2,1)S(1)} %copy-done.1), custom_call_target="tpu_custom_call" | custom-call | tf_op jit(solution)/shard_map/pallas_call | solution.py:206
  178.1 16.3 %all-to-all-start.1 = ((bf16[16,16,2048]{2,1,0:T(8,128)(2,1)}), bf16[16,16,2048]{2,1,0:T(8,128)(2,1)}, u32[]{:S(2)}, u32[]{:S(2)}) async-start(bf16[16,16,2048]{2,1,0:T(8,128)(2,1)} %copy-done.6), calls=%async_computation.1 | async-start | bytes 2097152 | tf_op jit(solution)/shard_map/all_to_all | solution.py:323
  194.4 3.9 fusion.29
  198.3 19.1 %all-to-all-done.1 = bf16[16,16,2048]{2,1,0:T(8,128)(2,1)} async-done(((bf16[16,16,2048]{2,1,0:T(8,128)(2,1)}), bf16[16,16,2048]{2,1,0:T(8,128)(2,1)}, u32[]{:S(2)}, u32[]{:S(2)}) %all-to-all-start.1) | async-done | bytes 1048608 | tf_op jit(solution)/shard_map/all_to_all | solution.py:323
  225.7 23.5 %shard_map.140.x_ref = bf16[16,16,2048]{2,1,0:T(8,128)(2,1)} custom-call(bf16[16,16,2048]{2,1,0:T(8,128)(2,1)} %bitcast.315), custom_call_target="tpu_custom_call" | custom-call | tf_op jit(solution)/shard_map/pallas_call | solution.py:271
  251.7 6.9 %shard_map.141 = bf16[16,16,4096]{2,1,0:T(8,128)(2,1)} custom-call(bf16[16,16,2048]{2,1,0:T(8,128)(2,1)S(1)} %copy-done.2, bf16[8,256,256]{2,1,0:T(8,128)(2,1)S(1)} %get-tuple-element.14.left_ref, bf16[8,256,256]{2,1,0:T(8,128)(2,1)S(1)} %copy-done.5), custom_call_target="tpu_custom_call" | custom-call | tf_op jit(solution)/shard_map/pallas_call | solution.py:206
  258.6 11.1 %all-to-all-start.2 = ((bf16[16,16,4096]{2,1,0:T(8,128)(2,1)}), bf16[16,16,4096]{2,1,0:T(8,128)(2,1)}, u32[]{:S(2)}, u32[]{:S(2)}) async-start(bf16[16,16,4096]{2,1,0:T(8,128)(2,1)} %shard_map.141), calls=%async_computation.2 | async-start | bytes 4194304 | tf_op jit(solution)/shard_map/all_to_all | solution.py:323
  277.3 33.5 %all-to-all-done.2 = bf16[16,16,4096]{2,1,0:T(8,128)(2,1)} async-done(((bf16[16,16,4096]{2,1,0:T(8,128)(2,1)}), bf16[16,16,4096]{2,1,0:T(8,128)(2,1)}, u32[]{:S(2)}, u32[]{:S(2)}) %all-to-all-start.2) | async-done | bytes 2097184 | tf_op jit(solution)/shard_map/all_to_all | solution.py:323
  310.8 4.0 fusion.74
  320.6 5.6 %multiply_convert_fusion.11 = (bf16[128,4096]{0,1:T(8,128)(2,1)S(1)}, bf16[128,4096]{0,1:T(8,128)(2,1)S(1)}, bf16[128,4096]{0,1:T(8,128)(2,1)S(1)}, bf16[128,4096]{0,1:T(8,128)(2,1)S(1)}) fusion(f32[128,4096]{0,1:T(8,128)} %copy.38, f32[4096]{0:T(1024)S(1)} %mul.382, f32[512,4096]{0,1:T(8,128)} %copy-done.7, f32[128,4096]{0,1:T(8,128)} %copy.40), kind=kLoop, calls=%fused_computation.112 | loop fusion | flops 11010048 | bytes 16793600 | tf_op jit(solution)/shard_map/convert.26
  331.8 4.3 fusion.28
  339.2 27.9 %shard_map.142.x_ref = bf16[16,16,2048]{2,1,0:T(8,128)(2,1)} custom-call(bf16[16,16,2048]{2,1,0:T(8,128)(2,1)} %bitcast.316), custom_call_target="tpu_custom_call" | custom-call | tf_op jit(solution)/shard_map/pallas_call | solution.py:271
  368.3 7.0 %shard_map.143 = bf16[16,16,4096]{2,1,0:T(8,128)(2,1)} custom-call(bf16[16,16,2048]{2,1,0:T(8,128)(2,1)S(1)} %copy-done.3, bf16[8,256,256]{2,1,0:T(8,128)(2,1)S(1)} %get-tuple-element.16.left_ref, bf16[8,256,256]{2,1,0:T(8,128)(2,1)S(1)} %get-tuple-element.17.right_ref), custom_call_target="tpu_custom_call" | custom-call | tf_op jit(solution)/shard_map/pallas_call | solution.py:206
  375.3 11.1 %all-to-all-start.3 = ((bf16[16,16,4096]{2,1,0:T(8,128)(2,1)}), bf16[16,16,4096]{2,1,0:T(8,128)(2,1)}, u32[]{:S(2)}, u32[]{:S(2)}) async-start(bf16[16,16,4096]{2,1,0:T(8,128)(2,1)} %shard_map.143), calls=%async_computation.3 | async-start | bytes 4194304 | tf_op jit(solution)/shard_map/all_to_all | solution.py:323
  386.4 3.6 fusion.123
  392.0 3.3 fusion.83
  397.4 30.1 %all-to-all-done.3 = bf16[16,16,4096]{2,1,0:T(8,128)(2,1)} async-done(((bf16[16,16,4096]{2,1,0:T(8,128)(2,1)}), bf16[16,16,4096]{2,1,0:T(8,128)(2,1)}, u32[]{:S(2)}, u32[]{:S(2)}) %all-to-all-start.3) | async-done | bytes 2097184 | tf_op jit(solution)/shard_map/all_to_all | solution.py:323
  427.5 3.3 fusion.72
  435.6 5.7 %multiply_convert_fusion.5 = (bf16[128,4096]{0,1:T(8,128)(2,1)S(1)}, bf16[128,4096]{0,1:T(8,128)(2,1)S(1)}, bf16[128,4096]{0,1:T(8,128)(2,1)S(1)}, bf16[128,4096]{0,1:T(8,128)(2,1)S(1)}) fusion(f32[128,4096]{0,1:T(8,128)} %copy.43, f32[4096]{0:T(1024)S(1)} %mul.382, f32[512,4096]{0,1:T(8,128)} %copy-done.8, f32[128,4096]{0,1:T(8,128)} %copy.45), kind=kLoop, calls=%fused_computation.104 | loop fusion | flops 11010048 | bytes 16793600 | tf_op jit(solution)/shard_map/convert.22
  443.7 3.5 fusion.44
  448.4 11.2 %all-to-all-start.4 = ((bf16[16,97,128]{2,1,0:T(8,128)(2,1)}), bf16[16,97,128]{2,1,0:T(8,128)(2,1)S(1)}, u32[]{:S(2)}, u32[]{:S(2)}) async-start(bf16[16,97,128]{2,1,0:T(8,128)(2,1)} %reshape.327), calls=%async_computation.4 | async-start | bytes 851968 | tf_op jit(solution)/shard_map/all_to_all | solution.py:323
  459.6 12.7 %all-to-all-done.4 = bf16[16,97,128]{2,1,0:T(8,128)(2,1)S(1)} async-done(((bf16[16,97,128]{2,1,0:T(8,128)(2,1)}), bf16[16,97,128]{2,1,0:T(8,128)(2,1)S(1)}, u32[]{:S(2)}, u32[]{:S(2)}) %all-to-all-start.4) | async-done | bytes 397344 | tf_op jit(solution)/shard_map/all_to_all | solution.py:323
  473.2 3.7 all-to-all-start.5
  476.9 9.1 %fusion.59 = bf16[4096,128]{1,0:T(8,128)(2,1)} fusion(bf16[64,64,128]{2,1,0:T(8,128)(2,1)S(1)} %copy-done.10, f32[4096,128]{1,0:T(8,128)} %get-tuple-element.92, f32[4096,128]{1,0:T(8,128)} %fusion.9, f32[4096,128]{1,0:T(8,128)} %get-tuple-element.86, f32[4096,128]{1,0:T(8,128)} %copy-done.20, f32[4096]{0:T(1024)S(1)} %broadcast_multiply_fusion.3, ...), kind=kLoop, calls=%fused_computation.95 | loop fusion | flops 13107200 | bytes 11666432 | tf_op jit(solution)/shard_map/convert_element_type | solution.py:452
  486.0 3.6 all-to-all-done.5
  (248 shorter events, 91.6 us)
Async XLA Ops:
  0.6 5.2 %copy-start.83 = (f32[2,128]{1,0:T(2,128)S(1)}, f32[2,128]{1,0:T(2,128)}, u32[]{:S(2)}) copy-start(f32[2,128]{1,0:T(2,128)} %param.13) | copy-start | bytes 3076
  2.6 6.0 %copy-start.43 = (bf16[2,128,512]{2,1,0:T(8,128)(2,1)S(1)}, bf16[2,128,512]{2,1,0:T(8,128)(2,1)}, u32[]{:S(2)}) copy-start(bf16[2,128,512]{2,1,0:T(8,128)(2,1)} %param.14) | copy-start | bytes 786436
  61.0 23.1 %copy-start.82 = (f32[2,128]{1,0:T(2,128)S(1)}, f32[2,128]{1,0:T(2,128)}, u32[]{:S(2)}) copy-start(f32[2,128]{1,0:T(2,128)} %param.16) | copy-start | bytes 3076
  61.0 25.0 %copy-start.60 = (bf16[2,128,128]{2,1,0:T(8,128)(2,1)S(1)}, bf16[2,128,128]{2,1,0:T(8,128)(2,1)}, u32[]{:S(2)}) copy-start(bf16[2,128,128]{2,1,0:T(8,128)(2,1)} %param.15) | copy-start | bytes 196612
  67.6 39.5 %all-to-all-start = ((bf16[16,16,2048]{2,1,0:T(8,128)(2,1)}), bf16[16,16,2048]{2,1,0:T(8,128)(2,1)}, u32[]{:S(2)}, u32[]{:S(2)}) async-start(bf16[16,16,2048]{2,1,0:T(8,128)(2,1)} %get-tuple-element.12), calls=%async_computation | async-start | bytes 2097152 | tf_op jit(solution)/shard_map/all_to_all | solution.py:323
  89.3 23.8 %copy-start.44 = (bf16[2,128,128]{2,1,0:T(8,128)(2,1)S(1)}, bf16[2,128,128]{2,1,0:T(8,128)(2,1)}, u32[]{:S(2)}) copy-start(bf16[2,128,128]{2,1,0:T(8,128)(2,1)} %param.17) | copy-start | bytes 196612
  107.1 4.4 copy-start.67
  107.1 5.9 %copy-start.17 = (f32[4096,128]{1,0:T(8,128)S(1)}, f32[4096,128]{1,0:T(8,128)}, u32[]{:S(2)}) copy-start(f32[4096,128]{1,0:T(8,128)} %fusion.9) | copy-start | bytes 6291460
  178.1 39.3 %all-to-all-start.1 = ((bf16[16,16,2048]{2,1,0:T(8,128)(2,1)}), bf16[16,16,2048]{2,1,0:T(8,128)(2,1)}, u32[]{:S(2)}, u32[]{:S(2)}) async-start(bf16[16,16,2048]{2,1,0:T(8,128)(2,1)} %copy-done.6), calls=%async_computation.1 | async-start | bytes 2097152 | tf_op jit(solution)/shard_map/all_to_all | solution.py:323
  258.6 11.1 %copy-start.80 = (f32[128]{0:T(128)S(1)}, f32[128]{0:T(128)}, u32[]{:S(2)}) copy-start(f32[128]{0:T(128)} %get-tuple-element.30) | copy-start | bytes 1540
  258.6 11.2 %copy-start.66 = (f32[1,16,2,128]{3,2,1,0:T(2,128)S(1)}, f32[1,16,2,128]{3,2,1,0:T(2,128)}, u32[]{:S(2)}) copy-start(f32[1,16,2,128]{3,2,1,0:T(2,128)} %get-tuple-element.72) | copy-start | bytes 49156
  258.6 11.8 %copy-start.65 = (f32[1,16,2,128]{3,2,1,0:T(2,128)S(1)}, f32[1,16,2,128]{3,2,1,0:T(2,128)}, u32[]{:S(2)}) copy-start(f32[1,16,2,128]{3,2,1,0:T(2,128)} %get-tuple-element.74) | copy-start | bytes 49156
  258.6 52.2 %all-to-all-start.2 = ((bf16[16,16,4096]{2,1,0:T(8,128)(2,1)}), bf16[16,16,4096]{2,1,0:T(8,128)(2,1)}, u32[]{:S(2)}, u32[]{:S(2)}) async-start(bf16[16,16,4096]{2,1,0:T(8,128)(2,1)} %shard_map.141), calls=%async_computation.2 | async-start | bytes 4194304 | tf_op jit(solution)/shard_map/all_to_all | solution.py:323
  269.7 4.3 copy-start.55
  269.7 4.3 copy-start.63
  271.0 4.6 copy-start.24
  271.0 4.6 copy-start.35
  331.7 4.4 copy-start.20
  331.7 4.4 copy-start.56
  331.7 4.3 copy-start.58
  331.8 4.3 copy-start.13
  331.8 4.3 copy-start.49
  331.8 4.3 copy-start.51
  375.3 11.1 %copy-start.70 = (f32[128]{0:T(128)S(1)}, f32[128]{0:T(128)}, u32[]{:S(2)}) copy-start(f32[128]{0:T(128)} %get-tuple-element.82) | copy-start | bytes 1540
  375.3 52.3 %all-to-all-start.3 = ((bf16[16,16,4096]{2,1,0:T(8,128)(2,1)}), bf16[16,16,4096]{2,1,0:T(8,128)(2,1)}, u32[]{:S(2)}, u32[]{:S(2)}) async-start(bf16[16,16,4096]{2,1,0:T(8,128)(2,1)} %shard_map.143), calls=%async_computation.3 | async-start | bytes 4194304 | tf_op jit(solution)/shard_map/all_to_all | solution.py:323
  435.6 5.7 %copy-start.23 = (bf16[128,4096]{0,1:T(8,128)(2,1)S(1)}, bf16[128,4096]{0,1:T(8,128)(2,1)}, u32[]{:S(2)}) copy-start(bf16[128,4096]{0,1:T(8,128)(2,1)} %copy-done.21) | copy-start | bytes 3145732
  447.4 29.5 %copy-start.26 = (bf16[64,64,128]{2,1,0:T(8,128)(2,1)S(1)}, bf16[64,64,128]{2,1,0:T(8,128)(2,1)}, u32[]{:S(2)}) copy-start(bf16[64,64,128]{2,1,0:T(8,128)(2,1)} %param.10) | copy-start | bytes 3145732
  447.4 29.5 %copy-start.57 = (f32[4096]{0:T(1024)S(1)}, f32[4096]{0:T(1024)}, u32[]{:S(2)}) copy-start(f32[4096]{0:T(1024)} %copy-done.56) | copy-start | bytes 49156
  447.4 29.5 %copy-start.59 = (f32[4096]{0:T(1024)S(1)}, f32[4096]{0:T(1024)}, u32[]{:S(2)}) copy-start(f32[4096]{0:T(1024)} %copy-done.58) | copy-start | bytes 49156
  447.4 29.5 %copy-start.71 = (f32[128]{0:T(128)S(1)}, f32[128]{0:T(128)}, u32[]{:S(2)}) copy-start(f32[128]{0:T(128)} %get-tuple-element.82) | copy-start | bytes 1540
  448.4 23.9 %all-to-all-start.4 = ((bf16[16,97,128]{2,1,0:T(8,128)(2,1)}), bf16[16,97,128]{2,1,0:T(8,128)(2,1)S(1)}, u32[]{:S(2)}, u32[]{:S(2)}) async-start(bf16[16,97,128]{2,1,0:T(8,128)(2,1)} %reshape.327), calls=%async_computation.4 | async-start | bytes 851968 | tf_op jit(solution)/shard_map/all_to_all | solution.py:323
  473.2 16.4 %all-to-all-start.5 = ((bf16[16,97,128]{2,1,0:T(8,128)(2,1)}), bf16[16,97,128]{2,1,0:T(8,128)(2,1)S(1)}, u32[]{:S(2)}, u32[]{:S(2)}) async-start(bf16[16,97,128]{2,1,0:T(8,128)(2,1)} %broadcast_in_dim.14), calls=%async_computation.5 | async-start | bytes 851968 | tf_op jit(solution)/shard_map/all_to_all | solution.py:323
  (58 other events, 140.7 us)
